TPU v7x, 32 devices: a whole 2x2x4 slice. The times are simulated.
32 devices in a mesh: energy: 8 (over y, x, core), mom: 4 (over z).
Axes of the slice: x: 2, y: 2, z: 4, core: 2. Of those that a mesh axis runs over, the one named last changes fastest.
Arguments:
- green_ret: bfloat16 [8, 4, 12, 3, 2, 128, 128], P('energy', 'mom'), may hold values from -0.5 to 0.5
- sigma_in: bfloat16 [8, 4, 12, 2, 128, 128], P('energy', 'mom'), may hold values from -6 to 6
- coupling: bfloat16 [4, 128, 128], replicated, may hold values from -0.5 to 0.5
- pattern: int32 [12], replicated, may hold values from 0 to 3
- neighbours: int32 [4, 3], P('mom'), may hold values from -1 to 1
- offsets: int32 [32], replicated, may hold values from -8 to 8, as said below
- tap_weight: float32 [32], replicated, may hold values from 0.005 to 0.04
Outputs:
- self_energy: bfloat16 [8, 4, 2, 1536, 128], P(None, 'mom', None, 'energy')
Inputs may be any that keep to these rules, and one draw needn't show every extreme that they name: `offsets`: both ends of the range are taken by some tap.
All inputs are finite; a program needn't handle non-finite values.
Results may differ from a plain program's by a relative error of at most 0.0081.
Values may be sent and summed in bfloat16 or wider, within the bound.
A program may use at most 64 MiB of HBM per device.

v0:
```python
import jax
import jax.numpy as jnp
from jax import lax
from jax.sharding import PartitionSpec as P


def shifted(value, axis, steps):
    count = lax.axis_size(axis)
    pairs = [(source, (source + steps) % count) for source in range(count)]
    return lax.ppermute(value, axis, pairs)


def batched(left, right):
    return jnp.einsum("sab,sbc->sac", left, right, preferred_element_type=jnp.float32)


def batched_adjoint(left, right):
    return jnp.einsum("sab,scb->sac", left, right, preferred_element_type=jnp.float32)


def slab_lesser(green, padded, slab_coupling, first, last):
    orbitals = green.shape[-1]
    count = last - first
    couple = slab_coupling[first:last]
    total_real = jnp.zeros((count, orbitals, orbitals), jnp.float32)
    total_imag = jnp.zeros((count, orbitals, orbitals), jnp.float32)
    for term in range(3):
        near = padded[first + term : last + term]
        block = green[first:last, term]
        coupled_real = batched(couple, block[:, 0]).astype(jnp.bfloat16)
        coupled_imag = batched(couple, block[:, 1]).astype(jnp.bfloat16)
        left_real = (batched(coupled_real, near[:, 0]) - batched(coupled_imag, near[:, 1])).astype(
            jnp.bfloat16
        )
        left_imag = (batched(coupled_real, near[:, 1]) + batched(coupled_imag, near[:, 0])).astype(
            jnp.bfloat16
        )
        total_real = (
            total_real
            + batched_adjoint(left_real, coupled_real)
            + batched_adjoint(left_imag, coupled_imag)
        )
        total_imag = (
            total_imag
            + batched_adjoint(left_imag, coupled_real)
            - batched_adjoint(left_real, coupled_imag)
        )
    rows = count * orbitals
    return jnp.stack(
        [total_real.reshape(rows, orbitals), total_imag.reshape(rows, orbitals)]
    ).astype(jnp.bfloat16)


def shards(green_ret, sigma_in, coupling, pattern, neighbours, offsets, tap_weight):
    e_local = green_ret.shape[0]
    energies = e_local * lax.axis_size("energy")
    slabs = green_ret.shape[2]
    half = slabs // 2
    kinds = coupling.shape[0]
    onehot = (pattern[:, None] == jnp.arange(kinds, dtype=jnp.int32)[None, :]).astype(jnp.bfloat16)
    slab_coupling = jnp.dot(onehot, coupling.reshape(kinds, -1), preferred_element_type=jnp.float32)
    slab_coupling = slab_coupling.astype(jnp.bfloat16).reshape(
        slabs, coupling.shape[1], coupling.shape[2]
    )
    weights = [jnp.sum((neighbours[0] == side).astype(jnp.float32)) for side in (-1, 0, 1)]
    index = jnp.arange(energies, dtype=jnp.int32)
    hit = index[None, :, None] == index[:, None, None] - offsets[None, None, :]
    banded = jnp.sum(
        jnp.where(hit, tap_weight[None, None, :], jnp.zeros((), jnp.float32)), axis=2
    ).astype(jnp.bfloat16)
    green = green_ret[0, 0]
    padded = jnp.pad(sigma_in[0, 0], ((1, 1), (0, 0), (0, 0), (0, 0)))
    pieces = []
    for first in (0, half):
        piece = slab_lesser(green, padded, slab_coupling, first, first + half)
        below = shifted(piece, "mom", 1)
        above = shifted(piece, "mom", -1)
        total = weights[0] * below.astype(jnp.float32) + weights[1] * piece.astype(jnp.float32)
        pieces.append((total + weights[2] * above.astype(jnp.float32)).astype(jnp.bfloat16))
    mixed_parts = [jnp.concatenate(pieces, axis=1)]
    mixed = jnp.stack(mixed_parts)
    result = jnp.einsum(
        "ef,fcrk->ecrk",
        banded,
        lax.all_to_all(mixed, "energy", split_axis=2, concat_axis=0, tiled=True),
        preferred_element_type=jnp.float32,
    ).astype(jnp.bfloat16)
    return result[:, None]


def solution(mesh):
    return jax.shard_map(
        shards,
        mesh=mesh,
        in_specs=(
            P("energy", "mom", None, None, None, None, None),
            P("energy", "mom", None, None, None, None),
            P(),
            P(),
            P("mom", None),
            P(),
            P(),
        ),
        out_specs=P(None, "mom", None, "energy", None),
        check_vma=False,
    )
```

profile of v0, /device:TPU:0, one launch (start us, length us, event | category | flops | bytes accessed | tf_op | source)
XLA Modules:
  0.0 78.1 jit_solution(17315510375331789014)
XLA Ops:
  0.0 1.8 %copy.124 = bf16[1,1,12,3,2,128,128]{6,5,2,4,3,1,0:T(8,128)(2,1)S(1)} copy(bf16[1,1,12,3,2,128,128]{6,5,4,3,2,1,0:T(8,128)(2,1)} %param.7) | data formatting | bytes 4718592 | tf_op args[0]
  1.8 0.3 slice_bitcast_fusion.6
  2.1 0.6 copy-done.1
  2.7 0.3 convolution_convert_fusion
  8.2 0.3 convolution_add_fusion.8
  9.0 0.3 convolution_add_fusion.7
  9.2 0.3 convolution_add_fusion.5
  9.5 0.3 convolution_add_fusion
  9.8 0.3 fusion.16
  10.3 0.3 fusion.15
  10.6 5.1 %collective-permute-start.3 = (bf16[2,768,128]{2,1,0:T(8,128)(2,1)S(1)}, bf16[2,768,128]{2,1,0:T(8,128)(2,1)S(1)}, u32[]{:S(2)}, u32[]{:S(2)}) collective-permute-start(bf16[2,768,128]{2,1,0:T(8,128)(2,1)S(1)} %pad_maximum_fusion.1), channel_id=1, source_target_pairs={{0,3},{1,0},{2,1},{3,2},{4,7},{5,4},{6,5},{7,6},{8,11},{9,8},{10,9... | collective-permute-start | bytes 1179656 | tf_op jit(solution)/shard_map/ppermute | solution.py:10
  21.5 0.3 convolution_add_fusion.10
  22.7 3.9 %collective-permute-start.1 = (bf16[2,768,128]{2,1,0:T(8,128)(2,1)S(1)}, bf16[2,768,128]{2,1,0:T(8,128)(2,1)S(1)}, u32[]{:S(2)}, u32[]{:S(2)}) collective-permute-start(bf16[2,768,128]{2,1,0:T(8,128)(2,1)S(1)} %pad_maximum_fusion), channel_id=1, source_target_pairs={{0,3},{1,0},{2,1},{3,2},{4,7},{5,4},{6,5},{7,6},{8,11},{9,8},{10,9... | collective-permute-start | bytes 1179656 | tf_op jit(solution)/shard_map/ppermute | solution.py:10
  26.6 0.6 fusion.60
  27.2 7.4 %collective-permute-done.2 = bf16[2,768,128]{2,1,0:T(8,128)(2,1)S(1)} collective-permute-done((bf16[2,768,128]{2,1,0:T(8,128)(2,1)S(1)}, bf16[2,768,128]{2,1,0:T(8,128)(2,1)S(1)}, u32[]{:S(2)}, u32[]{:S(2)}) %collective-permute-start.2) | collective-permute-done | bytes 393248 | tf_op jit(solution)/shard_map/ppermute | solution.py:10
  34.6 2.1 %add_convert_fusion = bf16[2,768,128]{2,1,0:T(8,128)(2,1)S(1)} fusion(bf16[2,768,128]{2,1,0:T(8,128)(2,1)S(1)} %collective-permute-done.3, bf16[2,768,128]{2,1,0:T(8,128)(2,1)S(1)} %collective-permute-done.2, f32[]{:T(128)} %get-tuple-element.6, f32[]{:T(128)} %get-tuple-element.7, f32[]{:T(128)} %get-tuple-element.5, bf16[1,768,128]{2,1,0:T(8,128)(2,1)S(1)} %bitcast.254, ...), kind=kLoop, calls=%fused_computation.71 | loop fusion | flops 1966080 | bytes 1572876 | tf_op jit(solution)/shard_map/convert_element_type | solution.py:79
  36.7 5.5 %collective-permute-done.1 = bf16[2,768,128]{2,1,0:T(8,128)(2,1)S(1)} collective-permute-done((bf16[2,768,128]{2,1,0:T(8,128)(2,1)S(1)}, bf16[2,768,128]{2,1,0:T(8,128)(2,1)S(1)}, u32[]{:S(2)}, u32[]{:S(2)}) %collective-permute-start.1) | collective-permute-done | bytes 393248 | tf_op jit(solution)/shard_map/ppermute | solution.py:10
  42.1 8.2 %collective-permute-done = bf16[2,768,128]{2,1,0:T(8,128)(2,1)S(1)} collective-permute-done((bf16[2,768,128]{2,1,0:T(8,128)(2,1)S(1)}, bf16[2,768,128]{2,1,0:T(8,128)(2,1)S(1)}, u32[]{:S(2)}, u32[]{:S(2)}) %collective-permute-start) | collective-permute-done | bytes 393248 | tf_op jit(solution)/shard_map/ppermute | solution.py:10
  50.3 2.1 %add_convert_fusion.1 = bf16[2,768,128]{2,1,0:T(8,128)(2,1)S(1)} fusion(bf16[2,768,128]{2,1,0:T(8,128)(2,1)S(1)} %collective-permute-done.1, bf16[2,768,128]{2,1,0:T(8,128)(2,1)S(1)} %collective-permute-done, f32[]{:T(128)} %get-tuple-element.6, f32[]{:T(128)} %get-tuple-element.7, f32[]{:T(128)} %get-tuple-element.5, bf16[1,768,128]{2,1,0:T(8,128)(2,1)S(1)} %bitcast.258, ...), kind=kLoop, calls=%fused_computation.72 | loop fusion | flops 1966080 | bytes 1572876 | tf_op jit(solution)/shard_map/convert_element_type | solution.py:79
  52.5 7.3 %copy.55 = bf16[1,2,1536,128]{3,1,0,2:T(2,128)(2,1)} copy(bf16[1,2,1536,128]{3,2,1,0:T(8,128)(2,1)S(1)} %maximum_bitcast_fusion) | data formatting | bytes 1572864 | tf_op jit(solution)/shard_map/stack | solution.py:81
  59.7 3.7 %all-to-all-start = ((bf16[1,2,1536,128]{3,1,0,2:T(2,128)(2,1)}), bf16[1,2,1536,128]{3,1,0,2:T(2,128)(2,1)S(1)}, u32[]{:S(2)}, u32[]{:S(2)}) async-start(bf16[1,2,1536,128]{3,1,0,2:T(2,128)(2,1)} %copy.55), calls=%async_computation | async-start | bytes 1572864 | tf_op jit(solution)/shard_map/all_to_all | solution.py:85
  63.6 12.5 %all-to-all-done = bf16[1,2,1536,128]{3,1,0,2:T(2,128)(2,1)S(1)} async-done(((bf16[1,2,1536,128]{3,1,0,2:T(2,128)(2,1)}), bf16[1,2,1536,128]{3,1,0,2:T(2,128)(2,1)S(1)}, u32[]{:S(2)}, u32[]{:S(2)}) %all-to-all-start) | async-done | bytes 786464 | tf_op jit(solution)/shard_map/all_to_all | solution.py:85
  76.0 1.0 %fusion = bf16[8,1,2,192,128]{4,0,3,2,1:T(8,128)(2,1)S(1)} fusion(bf16[1,2,8,192,128]{4,1,3,2,0:T(2,128)(2,1)S(1)} %bitcast.252, bf16[8,8]{1,0:T(8,128)(2,1)S(1)} %select_reduce_fusion), kind=kOutput, calls=%fused_computation.3 | convolution fusion | flops 6684672 | bytes 1572992 | tf_op jit(solution)/shard_map/ef,fcrk->ecrk/dot_general | solution.py:82
  77.0 1.1 %copy.58 = bf16[8,1,2,192,128]{4,3,2,1,0:T(8,128)(2,1)} copy(bf16[8,1,2,192,128]{4,0,3,2,1:T(8,128)(2,1)S(1)} %fusion) | data formatting | bytes 1572864 | tf_op jit(solution)/shard_map/broadcast_in_dim | solution.py:88
  (75 shorter events, 12.4 us)
Async XLA Ops:
  1.8 0.9 %copy-start.1 = (bf16[4,128,128]{2,1,0:T(8,128)(2,1)S(1)}, bf16[4,128,128]{2,1,0:T(8,128)(2,1)}, u32[]{:S(2)}) copy-start(bf16[4,128,128]{2,1,0:T(8,128)(2,1)} %param.9) | copy-start | bytes 393220
  1.8 0.9 %copy-start.5 = (s32[12]{0:T(128)S(1)}, s32[12]{0:T(128)}, u32[]{:S(2)}) copy-start(s32[12]{0:T(128)} %param.10) | copy-start | bytes 148
  3.4 1.1 %copy-start = (bf16[1,1,12,2,128,128]{5,4,3,2,1,0:T(8,128)(2,1)S(1)}, bf16[1,1,12,2,128,128]{5,4,3,2,1,0:T(8,128)(2,1)}, u32[]{:S(2)}) copy-start(bf16[1,1,12,2,128,128]{5,4,3,2,1,0:T(8,128)(2,1)} %param.8) | copy-start | bytes 2359300
  10.6 16.5 %collective-permute-start.3 = (bf16[2,768,128]{2,1,0:T(8,128)(2,1)S(1)}, bf16[2,768,128]{2,1,0:T(8,128)(2,1)S(1)}, u32[]{:S(2)}, u32[]{:S(2)}) collective-permute-start(bf16[2,768,128]{2,1,0:T(8,128)(2,1)S(1)} %pad_maximum_fusion.1), channel_id=1, source_target_pairs={{0,3},{1,0},{2,1},{3,2},{4,7},{5,4},{6,5},{7,6},{8,11},{9,8},{10,9... | collective-permute-start | bytes 1179656 | tf_op jit(solution)/shard_map/ppermute | solution.py:10
  15.7 18.9 %collective-permute-start.2 = (bf16[2,768,128]{2,1,0:T(8,128)(2,1)S(1)}, bf16[2,768,128]{2,1,0:T(8,128)(2,1)S(1)}, u32[]{:S(2)}, u32[]{:S(2)}) collective-permute-start(bf16[2,768,128]{2,1,0:T(8,128)(2,1)S(1)} %pad_maximum_fusion.1), channel_id=1, source_target_pairs={{0,1},{1,2},{2,3},{3,0},{4,5},{5,6},{6,7},{7,4},{8,9},{9,10},{10,1... | collective-permute-start | bytes 1179656 | tf_op jit(solution)/shard_map/ppermute | solution.py:10
  22.1 4.5 %copy-start.3 = (s32[1,3]{1,0:T(1,128)S(1)}, s32[1,3]{1,0:T(1,128)}, u32[]{:S(2)}) copy-start(s32[1,3]{1,0:T(1,128)} %param.11) | copy-start | bytes 40
  22.7 19.5 %collective-permute-start.1 = (bf16[2,768,128]{2,1,0:T(8,128)(2,1)S(1)}, bf16[2,768,128]{2,1,0:T(8,128)(2,1)S(1)}, u32[]{:S(2)}, u32[]{:S(2)}) collective-permute-start(bf16[2,768,128]{2,1,0:T(8,128)(2,1)S(1)} %pad_maximum_fusion), channel_id=1, source_target_pairs={{0,3},{1,0},{2,1},{3,2},{4,7},{5,4},{6,5},{7,6},{8,11},{9,8},{10,9... | collective-permute-start | bytes 1179656 | tf_op jit(solution)/shard_map/ppermute | solution.py:10
  26.5 23.8 %collective-permute-start = (bf16[2,768,128]{2,1,0:T(8,128)(2,1)S(1)}, bf16[2,768,128]{2,1,0:T(8,128)(2,1)S(1)}, u32[]{:S(2)}, u32[]{:S(2)}) collective-permute-start(bf16[2,768,128]{2,1,0:T(8,128)(2,1)S(1)} %pad_maximum_fusion), channel_id=1, source_target_pairs={{0,1},{1,2},{2,3},{3,0},{4,5},{5,6},{6,7},{7,4},{8,9},{9,10},{10,1... | collective-permute-start | bytes 1179656 | tf_op jit(solution)/shard_map/ppermute | solution.py:10
  52.4 11.0 %copy-start.2 = (s32[32]{0:T(128)S(1)}, s32[32]{0:T(128)}, u32[]{:S(2)}) copy-start(s32[32]{0:T(128)} %param.12) | copy-start | bytes 388
  52.5 11.0 %copy-start.4 = (f32[32]{0:T(128)S(1)}, f32[32]{0:T(128)}, u32[]{:S(2)}) copy-start(f32[32]{0:T(128)} %param.13) | copy-start | bytes 388
  59.7 16.3 %all-to-all-start = ((bf16[1,2,1536,128]{3,1,0,2:T(2,128)(2,1)}), bf16[1,2,1536,128]{3,1,0,2:T(2,128)(2,1)S(1)}, u32[]{:S(2)}, u32[]{:S(2)}) async-start(bf16[1,2,1536,128]{3,1,0,2:T(2,128)(2,1)} %copy.55), calls=%async_computation | async-start | bytes 1572864 | tf_op jit(solution)/shard_map/all_to_all | solution.py:85
where the time goes:
time: 78.4 us; the launch traced here: 78.1 us
  waiting for transfers between devices  33.6 us (43%)
  matrix products  14.8 us (19%)
  starting transfers between devices  12.7 us (16%)
  local copies, waits for them, and re-layouts  11.6 us (15%)
  other arithmetic  4.95 us (6%)
    ppermute x4, waiting for transfers between devices, shifted(): return lax.ppermute(value, axis, pairs)  21.1 us
    all_to_all x1, waiting for transfers between devices, shards(): lax.all_to_all(mixed, 'energy', split_axis=2, concat_axis=0, tiled=True)  12.5 us
    ppermute x4, starting transfers between devices, shifted(): return lax.ppermute(value, axis, pairs)  8.98 us
    another operation x1, local copies, waits for them, and re-layouts, shards(): mixed = jnp.stack(mixed_parts)  7.26 us
    dot_general x36, matrix products, batched(): jnp.einsum('sab,sbc->sac', left, right, preferred_element_type=jnp.float32)  7.14 us
    dot_general x24, matrix products, batched_adjoint(): jnp.einsum('sab,scb->sac', left, right, preferred_element_type=jnp.float32)  6.33 us
    convert_element_type x2, other arithmetic, shards(): (total + weights[2] * above.astype(jnp.float32)).astype(jnp.bfloat16)  4.11 us
    all_to_all x1, starting transfers between devices, shards(): lax.all_to_all(mixed, 'energy', split_axis=2, concat_axis=0, tiled=True)  3.71 us
  transfers between devices with their start and end apart: 5, of which 4 were waited for; matrix products, arithmetic and copies ran while one was open for 12% of the time, Pallas kernels for 0%

commit v1 on v0

--- a/solution.py
+++ b/solution.py
@@ -2,6 +2,11 @@
 import jax.numpy as jnp
 from jax import lax
 from jax.sharding import PartitionSpec as P
+from jax.lax import all_to_all, axis_size
+
+begin_array_all = lambda obj, net_axis: jnp.concatenate(
+    all_to_all(jnp.stack(jnp.split(obj, axis_size(net_axis), axis=2)), net_axis, 0, 0), axis=0
+)
 
 
 def shifted(value, axis, steps):
@@ -82,7 +87,7 @@
     result = jnp.einsum(
         "ef,fcrk->ecrk",
         banded,
-        lax.all_to_all(mixed, "energy", split_axis=2, concat_axis=0, tiled=True),
+        begin_array_all(mixed, "energy"),
         preferred_element_type=jnp.float32,
     ).astype(jnp.bfloat16)
     return result[:, None]

time: 78.4 us -> 75.9 us (0.968)
  local copies, waits for them, and re-layouts: 11.6 us -> 9.49 us
    another operation x1, local copies, waits for them, and re-layouts: 7.26 us -> 0.65 us  [jnp.stack(jnp.split(obj, axis_size(net_axis), axis=2))]
    unnamed x15 -> x22, local copies, waits for them, and re-layouts: 2.72 us -> 7.25 us
  transfers between devices with their start and end apart: 5 -> 5, of which waited for: 4 -> 4; matrix products, arithmetic and copies ran while one was open for 12% -> 13% of each run, Pallas kernels for 0% -> 0%
where the time goes in v1:
time: 75.9 us; the launch traced here: 75.6 us
  waiting for transfers between devices  33.6 us (44%)
  matrix products  14.3 us (19%)
  starting transfers between devices  12.7 us (17%)
  local copies, waits for them, and re-layouts  9.49 us (13%)
  other arithmetic  4.95 us (7%)
    ppermute x4, waiting for transfers between devices, shifted(): return lax.ppermute(value, axis, pairs)  21.1 us
    all_to_all x1, waiting for transfers between devices, all_to_all(jnp.stack(jnp.split(obj, axis_size(net_axis), axis=2)), net_ax...  12.5 us
    ppermute x4, starting transfers between devices, shifted(): return lax.ppermute(value, axis, pairs)  8.99 us
    unnamed x22, local copies, waits for them, and re-layouts  7.25 us
    dot_general x36, matrix products, batched(): jnp.einsum('sab,sbc->sac', left, right, preferred_element_type=jnp.float32)  7.15 us
    dot_general x24, matrix products, batched_adjoint(): jnp.einsum('sab,scb->sac', left, right, preferred_element_type=jnp.float32)  6.3 us
    convert_element_type x2, other arithmetic, shards(): (total + weights[2] * above.astype(jnp.float32)).astype(jnp.bfloat16)  4.11 us
    all_to_all x1, starting transfers between devices, all_to_all(jnp.stack(jnp.split(obj, axis_size(net_axis), axis=2)), net_ax...  3.72 us
  transfers between devices with their start and end apart: 5, of which 4 were waited for; matrix products, arithmetic and copies ran while one was open for 13% of the time, Pallas kernels for 0%

profile of v1, /device:TPU:0, one launch (start us, length us, event | category | flops | bytes accessed | tf_op | source)
XLA Modules:
  0.0 75.6 jit_solution(10535563582874585212)
XLA Ops:
  0.0 1.8 %copy.214 = bf16[1,1,12,3,2,128,128]{6,5,2,4,3,1,0:T(8,128)(2,1)S(1)} copy(bf16[1,1,12,3,2,128,128]{6,5,4,3,2,1,0:T(8,128)(2,1)} %param.7) | data formatting | bytes 4718592 | tf_op args[0]
  1.8 0.3 slice_bitcast_fusion.6
  2.1 0.6 copy-done.1
  2.7 0.3 convolution_convert_fusion
  10.6 5.1 %collective-permute-start.3 = (bf16[2,768,128]{2,1,0:T(8,128)(2,1)S(1)}, bf16[2,768,128]{2,1,0:T(8,128)(2,1)S(1)}, u32[]{:S(2)}, u32[]{:S(2)}) collective-permute-start(bf16[2,768,128]{2,1,0:T(8,128)(2,1)S(1)} %pad_maximum_fusion.1), channel_id=1, source_target_pairs={{0,3},{1,0},{2,1},{3,2},{4,7},{5,4},{6,5},{7,6},{8,11},{9,8},{10,9... | collective-permute-start | bytes 1179656 | tf_op jit(solution)/shard_map/ppermute | solution.py:15
  22.7 3.9 %collective-permute-start.1 = (bf16[2,768,128]{2,1,0:T(8,128)(2,1)S(1)}, bf16[2,768,128]{2,1,0:T(8,128)(2,1)S(1)}, u32[]{:S(2)}, u32[]{:S(2)}) collective-permute-start(bf16[2,768,128]{2,1,0:T(8,128)(2,1)S(1)} %pad_maximum_fusion), channel_id=1, source_target_pairs={{0,3},{1,0},{2,1},{3,2},{4,7},{5,4},{6,5},{7,6},{8,11},{9,8},{10,9... | collective-permute-start | bytes 1179656 | tf_op jit(solution)/shard_map/ppermute | solution.py:15
  26.6 0.6 fusion.68
  27.2 7.5 %collective-permute-done.2 = bf16[2,768,128]{2,1,0:T(8,128)(2,1)S(1)} collective-permute-done((bf16[2,768,128]{2,1,0:T(8,128)(2,1)S(1)}, bf16[2,768,128]{2,1,0:T(8,128)(2,1)S(1)}, u32[]{:S(2)}, u32[]{:S(2)}) %collective-permute-start.2) | collective-permute-done | bytes 393248 | tf_op jit(solution)/shard_map/ppermute | solution.py:15
  34.6 2.1 %add_convert_fusion = bf16[2,768,128]{2,1,0:T(8,128)(2,1)S(1)} fusion(bf16[2,768,128]{2,1,0:T(8,128)(2,1)S(1)} %collective-permute-done.3, bf16[2,768,128]{2,1,0:T(8,128)(2,1)S(1)} %collective-permute-done.2, f32[]{:T(128)} %get-tuple-element.6, f32[]{:T(128)} %get-tuple-element.7, f32[]{:T(128)} %get-tuple-element.5, bf16[1,768,128]{2,1,0:T(8,128)(2,1)S(1)} %bitcast.282, ...), kind=kLoop, calls=%fused_computation.71 | loop fusion | flops 1966080 | bytes 1572876 | tf_op jit(solution)/shard_map/convert_element_type | solution.py:84
  36.7 5.5 %collective-permute-done.1 = bf16[2,768,128]{2,1,0:T(8,128)(2,1)S(1)} collective-permute-done((bf16[2,768,128]{2,1,0:T(8,128)(2,1)S(1)}, bf16[2,768,128]{2,1,0:T(8,128)(2,1)S(1)}, u32[]{:S(2)}, u32[]{:S(2)}) %collective-permute-start.1) | collective-permute-done | bytes 393248 | tf_op jit(solution)/shard_map/ppermute | solution.py:15
  42.1 8.2 %collective-permute-done = bf16[2,768,128]{2,1,0:T(8,128)(2,1)S(1)} collective-permute-done((bf16[2,768,128]{2,1,0:T(8,128)(2,1)S(1)}, bf16[2,768,128]{2,1,0:T(8,128)(2,1)S(1)}, u32[]{:S(2)}, u32[]{:S(2)}) %collective-permute-start) | collective-permute-done | bytes 393248 | tf_op jit(solution)/shard_map/ppermute | solution.py:15
  50.3 2.1 %add_convert_fusion.1 = bf16[2,768,128]{2,1,0:T(8,128)(2,1)S(1)} fusion(bf16[2,768,128]{2,1,0:T(8,128)(2,1)S(1)} %collective-permute-done.1, bf16[2,768,128]{2,1,0:T(8,128)(2,1)S(1)} %collective-permute-done, f32[]{:T(128)} %get-tuple-element.6, f32[]{:T(128)} %get-tuple-element.7, f32[]{:T(128)} %get-tuple-element.5, bf16[1,768,128]{2,1,0:T(8,128)(2,1)S(1)} %bitcast.286, ...), kind=kLoop, calls=%fused_computation.72 | loop fusion | flops 1966080 | bytes 1572876 | tf_op jit(solution)/shard_map/convert_element_type | solution.py:84
  52.5 0.6 fusion.52
  53.1 0.6 fusion.51
  53.8 0.6 fusion.50
  54.4 0.6 fusion.49
  55.1 0.6 fusion.48
  55.7 0.6 fusion.47
  56.4 0.6 fusion.46
  57.0 0.6 fusion.45
  57.6 3.7 %all-to-all-start = ((bf16[8,1,2,192,128]{4,3,2,1,0:T(8,128)(2,1)}), bf16[8,1,2,192,128]{4,3,2,1,0:T(8,128)(2,1)S(1)}, u32[]{:S(2)}, u32[]{:S(2)}) async-start(bf16[8,1,2,192,128]{4,3,2,1,0:T(8,128)(2,1)} %fusion.45), calls=%async_computation | async-start | bytes 1572864 | tf_op jit(solution)/shard_map/all_to_all | solution.py:8
  61.5 12.5 %all-to-all-done = bf16[8,1,2,192,128]{4,3,2,1,0:T(8,128)(2,1)S(1)} async-done(((bf16[8,1,2,192,128]{4,3,2,1,0:T(8,128)(2,1)}), bf16[8,1,2,192,128]{4,3,2,1,0:T(8,128)(2,1)S(1)}, u32[]{:S(2)}, u32[]{:S(2)}) %all-to-all-start) | async-done | bytes 786464 | tf_op jit(solution)/shard_map/all_to_all | solution.py:8
  74.0 0.5 fusion
  74.5 1.0 %copy.150 = bf16[8,1,2,192,128]{4,3,2,1,0:T(8,128)(2,1)} copy(bf16[8,1,2,192,128]{4,0,3,2,1:T(8,128)(2,1)S(1)} %fusion) | data formatting | bytes 1572864 | tf_op jit(solution)/shard_map/broadcast_in_dim | solution.py:93
  (82 shorter events, 14.3 us)
Async XLA Ops:
  1.8 0.9 %copy-start.1 = (bf16[4,128,128]{2,1,0:T(8,128)(2,1)S(1)}, bf16[4,128,128]{2,1,0:T(8,128)(2,1)}, u32[]{:S(2)}) copy-start(bf16[4,128,128]{2,1,0:T(8,128)(2,1)} %param.9) | copy-start | bytes 393220
  1.8 0.9 %copy-start.5 = (s32[12]{0:T(128)S(1)}, s32[12]{0:T(128)}, u32[]{:S(2)}) copy-start(s32[12]{0:T(128)} %param.10) | copy-start | bytes 148
  3.4 1.1 %copy-start = (bf16[1,1,12,2,128,128]{5,4,3,2,1,0:T(8,128)(2,1)S(1)}, bf16[1,1,12,2,128,128]{5,4,3,2,1,0:T(8,128)(2,1)}, u32[]{:S(2)}) copy-start(bf16[1,1,12,2,128,128]{5,4,3,2,1,0:T(8,128)(2,1)} %param.8) | copy-start | bytes 2359300
  10.6 16.6 %collective-permute-start.3 = (bf16[2,768,128]{2,1,0:T(8,128)(2,1)S(1)}, bf16[2,768,128]{2,1,0:T(8,128)(2,1)S(1)}, u32[]{:S(2)}, u32[]{:S(2)}) collective-permute-start(bf16[2,768,128]{2,1,0:T(8,128)(2,1)S(1)} %pad_maximum_fusion.1), channel_id=1, source_target_pairs={{0,3},{1,0},{2,1},{3,2},{4,7},{5,4},{6,5},{7,6},{8,11},{9,8},{10,9... | collective-permute-start | bytes 1179656 | tf_op jit(solution)/shard_map/ppermute | solution.py:15
  15.7 18.9 %collective-permute-start.2 = (bf16[2,768,128]{2,1,0:T(8,128)(2,1)S(1)}, bf16[2,768,128]{2,1,0:T(8,128)(2,1)S(1)}, u32[]{:S(2)}, u32[]{:S(2)}) collective-permute-start(bf16[2,768,128]{2,1,0:T(8,128)(2,1)S(1)} %pad_maximum_fusion.1), channel_id=1, source_target_pairs={{0,1},{1,2},{2,3},{3,0},{4,5},{5,6},{6,7},{7,4},{8,9},{9,10},{10,1... | collective-permute-start | bytes 1179656 | tf_op jit(solution)/shard_map/ppermute | solution.py:15
  22.1 4.5 %copy-start.3 = (s32[1,3]{1,0:T(1,128)S(1)}, s32[1,3]{1,0:T(1,128)}, u32[]{:S(2)}) copy-start(s32[1,3]{1,0:T(1,128)} %param.11) | copy-start | bytes 40
  22.7 19.5 %collective-permute-start.1 = (bf16[2,768,128]{2,1,0:T(8,128)(2,1)S(1)}, bf16[2,768,128]{2,1,0:T(8,128)(2,1)S(1)}, u32[]{:S(2)}, u32[]{:S(2)}) collective-permute-start(bf16[2,768,128]{2,1,0:T(8,128)(2,1)S(1)} %pad_maximum_fusion), channel_id=1, source_target_pairs={{0,3},{1,0},{2,1},{3,2},{4,7},{5,4},{6,5},{7,6},{8,11},{9,8},{10,9... | collective-permute-start | bytes 1179656 | tf_op jit(solution)/shard_map/ppermute | solution.py:15
  26.5 23.8 %collective-permute-start = (bf16[2,768,128]{2,1,0:T(8,128)(2,1)S(1)}, bf16[2,768,128]{2,1,0:T(8,128)(2,1)S(1)}, u32[]{:S(2)}, u32[]{:S(2)}) collective-permute-start(bf16[2,768,128]{2,1,0:T(8,128)(2,1)S(1)} %pad_maximum_fusion), channel_id=1, source_target_pairs={{0,1},{1,2},{2,3},{3,0},{4,5},{5,6},{6,7},{7,4},{8,9},{9,10},{10,1... | collective-permute-start | bytes 1179656 | tf_op jit(solution)/shard_map/ppermute | solution.py:15
  52.4 8.9 %copy-start.2 = (s32[32]{0:T(128)S(1)}, s32[32]{0:T(128)}, u32[]{:S(2)}) copy-start(s32[32]{0:T(128)} %param.12) | copy-start | bytes 388
  52.5 8.9 %copy-start.4 = (f32[32]{0:T(128)S(1)}, f32[32]{0:T(128)}, u32[]{:S(2)}) copy-start(f32[32]{0:T(128)} %param.13) | copy-start | bytes 388
  57.6 16.3 %all-to-all-start = ((bf16[8,1,2,192,128]{4,3,2,1,0:T(8,128)(2,1)}), bf16[8,1,2,192,128]{4,3,2,1,0:T(8,128)(2,1)S(1)}, u32[]{:S(2)}, u32[]{:S(2)}) async-start(bf16[8,1,2,192,128]{4,3,2,1,0:T(8,128)(2,1)} %fusion.45), calls=%async_computation | async-start | bytes 1572864 | tf_op jit(solution)/shard_map/all_to_all | solution.py:8
